TPU v7x, 512 devices: a whole 4x4x16 slice. The times are simulated.
512 devices in a mesh: batch: 8 (over x, core), seq: 64 (over z, y).
Axes of the slice: x: 4, y: 4, z: 16, core: 2. Of those that a mesh axis runs over, the one named last changes fastest.
Arguments:
- query_nope: bfloat16 [8, 2, 16384], P('batch', None, 'seq'), may hold values from -6 to 6
- query_rope: bfloat16 [8, 2, 8192], P('batch', None, 'seq'), may hold values from -10 to 10
- latent_cache: bfloat16 [8, 65536, 576], P('batch', 'seq'), may hold values from -10 to 10
- lengths: int32 [8], P('batch'), may hold values from 16384 to 65536
- key_up: bfloat16 [128, 128, 512], P('seq', 'batch'), may hold values from -0.5 to 0.5
- value_up: bfloat16 [128, 512, 128], P('seq', 'batch'), may hold values from -1.5 to 1.5
Outputs:
- attended: bfloat16 [8, 2, 16384], P('batch', None, 'seq')
All inputs are finite; a program needn't handle non-finite values.
Results may differ from a plain program's by a relative error of at most 0.04.
Values may be sent and summed in bfloat16 or wider, within the bound.
No kernel may reach another device: no remote copies, remote signals or barrier semaphores. Data moves between devices by JAX's collectives and lax.ppermute only.
A program may use at most 128 MiB of HBM per device.

v0:
```python
import math

import jax
import jax.numpy as jnp
from jax import lax
from jax.sharding import PartitionSpec as P


def body(query_nope, query_rope, latent_cache, lengths, key_up, value_up):
    full_key, full_value = (
        lax.all_gather(key_up, "batch", axis=1, tiled=True),
        lax.all_gather(value_up, "batch", axis=1, tiled=True),
    )
    local_heads = full_key.shape[0]
    head_width = full_key.shape[1]
    latent_width = full_key.shape[2]
    row_count = query_nope.shape[0]
    query_count = query_nope.shape[1]
    rope_width = query_rope.shape[2] // local_heads
    query_width = latent_width + rope_width
    nope_query = query_nope.reshape(row_count, query_count, local_heads, head_width)
    absorbed = jnp.einsum(
        "rthn,hnl->rthl", nope_query, full_key, preferred_element_type=jnp.float32
    ).astype(jnp.bfloat16)
    rotary = query_rope.reshape(row_count, query_count, local_heads, rope_width)
    local_query = jnp.concatenate([absorbed, rotary], axis=-1).reshape(
        row_count, query_count, local_heads * query_width
    )
    all_query = lax.all_gather(local_query, "seq", axis=2, tiled=True).reshape(
        row_count, query_count, -1, query_width
    )
    block_len = latent_cache.shape[1]
    scale = 1.0 / math.sqrt(head_width + rope_width)
    scores = (
        jnp.einsum("rthd,rcd->rthc", all_query, latent_cache, preferred_element_type=jnp.float32)
        * scale
    )
    first_pos = lax.axis_index("seq") * block_len
    positions = first_pos + jnp.arange(block_len, dtype=jnp.int32)
    limits = lengths[:, None] - query_count + 1 + jnp.arange(query_count, dtype=jnp.int32)[None, :]
    visible = positions[None, None, None, :] < limits[:, :, None, None]
    scores = jnp.where(visible, scores, -1e30)
    local_max = jnp.max(scores, axis=-1)
    cache_values = latent_cache[:, :, :latent_width]
    global_max = lax.pmax(local_max, "seq")
    weights = jnp.where(visible, jnp.exp(scores - global_max[..., None]), 0.0)
    totals = jnp.sum(weights, axis=-1)
    summed = jnp.einsum(
        "rthc,rcl->rthl",
        weights.astype(jnp.bfloat16),
        cache_values,
        preferred_element_type=jnp.float32,
    )
    own_sums, own_totals = (
        lax.psum_scatter(summed, "seq", scatter_dimension=2, tiled=True),
        lax.psum_scatter(totals, "seq", scatter_dimension=2, tiled=True),
    )
    latent_out = (own_sums / own_totals[..., None]).astype(jnp.bfloat16)
    attended = jnp.einsum(
        "rthl,hlv->rthv", latent_out, full_value, preferred_element_type=jnp.float32
    )
    return attended.astype(jnp.bfloat16).reshape(row_count, query_count, local_heads * head_width)


def solution(mesh):
    in_specs = (
        P("batch", None, "seq"),
        P("batch", None, "seq"),
        P("batch", "seq", None),
        P("batch"),
        P("seq", "batch", None),
        P("seq", "batch", None),
    )
    out_specs = P("batch", None, "seq")
    return jax.shard_map(body, mesh=mesh, in_specs=in_specs, out_specs=out_specs, check_vma=False)
```

profile of v0, /device:TPU:2, one launch (start us, length us, event | category | flops | bytes accessed | tf_op | source)
XLA Modules:
  0.0 533.5 jit_solution(14605920627988984809)
XLA Ops:
  6.5 0.0 copy-start
  6.5 0.0 all-reduce.4.cloned.1.call-start
  7.3 15.8 %all_gather.9 = bf16[2,128,512]{2,1,0:T(8,128)(2,1)S(1)} all-gather(bf16[2,16,512]{2,1,0:T(8,128)(2,1)} %param.10), channel_id=1, replica_groups=mesh['batch'=8,'seq'=64] {'batch'}, dimensions={1}, use_global_device_ids=true | all-gather | bytes 294912 | tf_op jit(solution)/shard_map/all_gather | solution.py:11
  23.1 0.7 reshape.101
  23.9 0.0 copy-done
  23.9 0.1 fusion.2
  24.0 0.1 reshape.102
  24.1 98.5 %all_gather.10 = bf16[1,2,73728]{2,1,0:T(2,128)(2,1)S(1)} all-gather(bf16[1,2,1152]{2,1,0:T(2,128)(2,1)S(1)} %reshape.102), channel_id=1, replica_groups=mesh['batch'=8,'seq'=64] {'seq'}, dimensions={2}, use_global_device_ids=true | all-gather | bytes 299520 | tf_op jit(solution)/shard_map/all_gather | solution.py:29
  122.6 0.3 reshape.103
  123.0 0.1 broadcast_compare_fusion
  123.0 0.0 copy-done.2
  123.0 0.7 fusion.17
  123.7 140.4 %pmax.7 = f32[2,128]{1,0:T(2,128)S(1)} all-reduce(f32[2,128]{1,0:T(2,128)S(1)} %get-tuple-element.5), channel_id=1, replica_groups=mesh['batch'=8,'seq'=64] {'seq'}, use_global_device_ids=true, to_apply=%region_1.2 | all-reduce | flops 256 | bytes 2048 | tf_op jit(solution)/shard_map/pmax | solution.py:45
  264.1 1.3 convolution_bitcast_fusion
  265.4 0.0 all-reduce.4.cloned.1.call-update
  265.4 1.3 dynamic-slice
  267.4 0.3 fusion.6
  267.7 138.1 %all-reduce.1 = f32[1,2,128]{2,1,0:T(2,128)S(1)} all-reduce(f32[1,2,128]{2,1,0:T(2,128)S(1)} %bitcast.42), channel_id=3, replica_groups=mesh['batch'=8,'seq'=64] {'seq'}, use_global_device_ids=true, to_apply=%region_4.5.clone | all-reduce | flops 256 | bytes 2048
  405.8 0.1 dynamic-slice_bitcast_fusion
  405.9 0.0 copy-done.1
  405.9 12.8 %all_gather.11 = bf16[2,512,128]{2,1,0:T(8,128)(2,1)S(1)} all-gather(bf16[2,64,128]{2,1,0:T(8,128)(2,1)S(1)} %copy-done.1), channel_id=1, replica_groups=mesh['batch'=8,'seq'=64] {'batch'}, dimensions={1}, use_global_device_ids=true | all-gather | bytes 294912 | tf_op jit(solution)/shard_map/all_gather | solution.py:12
  418.7 106.5 %all-reduce.4.cloned.1.call-done = f32[1,2,128,512]{3,2,1,0:T(8,128)} async-done(((f32[1,2,128,512]{3,2,1,0:T(8,128)}), f32[1,2,128,512]{3,2,1,0:T(8,128)}) %all-reduce.4.cloned.1.call-update) | async-done | bytes 524304
  525.1 0.8 fusion.14
  526.0 0.7 fusion.3
  (7 shorter events, 0.0 us)
Async XLA Ops:
  6.5 17.3 %copy-start = (bf16[1,2,256]{2,1,0:T(2,128)(2,1)S(1)}, bf16[1,2,256]{2,1,0:T(2,128)(2,1)}, u32[]{:S(2)}) copy-start(bf16[1,2,256]{2,1,0:T(2,128)(2,1)} %param.6) | copy-start | bytes 3076
  6.5 116.5 %copy-start.2 = (bf16[1,1024,576]{1,2,0:T(8,128)(2,1)S(1)}, bf16[1,1024,576]{1,2,0:T(8,128)(2,1)}, u32[]{:S(2)}) copy-start(bf16[1,1024,576]{1,2,0:T(8,128)(2,1)} %param.8) | copy-start | bytes 3538948
  6.5 518.6 %all-reduce.4.cloned.1.call-start = ((), (), s32[]{:S(2)}) async-start(), calls=%async_computation | async-start | bytes 1048576
  265.4 140.4 %copy-start.1 = (bf16[2,64,128]{2,1,0:T(8,128)(2,1)S(1)}, bf16[2,64,128]{2,1,0:T(8,128)(2,1)}, u32[]{:S(2)}) copy-start(bf16[2,64,128]{2,1,0:T(8,128)(2,1)} %param.11) | copy-start | bytes 98308
Sparse Core Ops, SparseCore 0:
  265.6 259.5 all-reduce.3
where the time goes:
time: 534 us
  blocking collectives  406 us (76%)
  waiting for transfers between devices  106 us (20%)
  between operations  14.8 us (3%)
    pmax x1, blocking collectives, body(): global_max = lax.pmax(local_max, 'seq')  140 us
    unnamed x1, blocking collectives  138 us
    unnamed x2, waiting for transfers between devices  106 us
    all_gather x1, blocking collectives, body(): lax.all_gather(local_query, 'seq', axis=2, tiled=True)  98.5 us
    all_gather x1, blocking collectives, body(): lax.all_gather(key_up, 'batch', axis=1, tiled=True)  15.8 us
    all_gather x1, blocking collectives, body(): lax.all_gather(value_up, 'batch', axis=1, tiled=True)  12.8 us
  transfers between devices with their start and end apart: 1, of which 1 were waited for; matrix products, arithmetic and copies ran while one was open for 0% of the time, Pallas kernels for 0%

commit v1 on v0

v1 whole, which is shorter than its diff:
```python
import functools
import math

import jax
import jax.numpy as jnp
from jax import lax
from jax.experimental import pallas as pl
from jax.experimental.pallas import tpu as pltpu
from jax.sharding import PartitionSpec as P

VMEM = pl.BlockSpec(memory_space=pltpu.VMEM)
SMEM = pl.BlockSpec(memory_space=pltpu.SMEM)
PARAMS = pltpu.CompilerParams(vmem_limit_bytes=24 * 1024 * 1024)
F32 = jnp.float32
BF16 = jnp.bfloat16
HIDDEN = -1e30


def split3(x):
    high = x.astype(BF16).astype(F32)
    rest = x - high
    mid = rest.astype(BF16).astype(F32)
    return high, mid, (rest - mid).astype(BF16).astype(F32)


def pack_kernel(key_ref, value_ref, out_ref):
    heads, depth, latent = key_ref.shape
    key = jnp.concatenate(
        [key_ref[:, :, c : c + 128].reshape(heads * depth, 128) for c in range(0, latent, 128)], 0
    )
    value = value_ref[...].reshape(-1, 128)
    both = jnp.concatenate([key, value], 0)
    for i in range(out_ref.shape[0]):
        out_ref[i] = both


def absorb_kernel(heads, latent, parts_ref, nope_ref, rope_ref, out_ref):
    tokens = nope_ref.shape[1]
    head_width = nope_ref.shape[2] // heads
    rope_width = rope_ref.shape[2] // heads
    groups = parts_ref.shape[0]
    depth = head_width // groups
    blocks = []
    for c in range(latent // 128):
        rows = [
            parts_ref[:, (c * heads + h) * depth : (c * heads + h + 1) * depth, :].reshape(
                head_width, 128
            )
            for h in range(heads)
        ]
        blocks.append(jnp.concatenate(rows, 0))
    keys = jnp.concatenate(blocks, 1)
    row = lax.broadcasted_iota(jnp.int32, (8, heads * head_width), 0)
    col = lax.broadcasted_iota(jnp.int32, (8, heads * head_width), 1)
    nope = nope_ref[0].astype(F32)
    spread = jnp.zeros(row.shape, F32)
    for t in range(tokens):
        spread = jnp.where(row // heads == t, nope[t : t + 1], spread)
    spread = jnp.where(row % heads == col // head_width, spread, 0.0)
    absorbed = jnp.dot(spread.astype(BF16), keys, preferred_element_type=F32)
    rope = rope_ref[0].astype(F32)
    row = lax.broadcasted_iota(jnp.int32, (8, 128), 0)
    col = lax.broadcasted_iota(jnp.int32, (8, 128), 1)
    turned = jnp.zeros(row.shape, F32)
    for t in range(tokens):
        for h in range(heads):
            moved = rope[t : t + 1]
            if h:
                moved = pltpu.roll(moved, 128 - h * rope_width, 1)
            turned = jnp.where(row == t * heads + h, moved, turned)
    turned = jnp.where(col < rope_width, turned, 0.0)
    local = jnp.concatenate([absorbed, turned], 1)[: tokens * heads]
    out_ref[...] = jnp.broadcast_to(local[None], out_ref.shape).astype(BF16)


def attend_kernel(heads, tokens, scale, latent, query_ref, cache_ref, length_ref, out_ref):
    rows = query_ref.shape[0]
    block_len, width = cache_ref.shape
    contract = (((1,), (1,)), ((), ()))
    scores = lax.dot_general(
        query_ref[:, :latent], cache_ref[:, :latent], contract, preferred_element_type=F32
    )
    scores += lax.dot_general(
        query_ref[:, latent:width], cache_ref[:, latent:width], contract, preferred_element_type=F32
    )
    scores = scores * scale
    limit = length_ref[0] - tokens + 1 - lax.axis_index("seq") * block_len
    row = lax.broadcasted_iota(jnp.int32, (rows, 1), 0)
    limits = limit + (row // heads) % tokens
    visible = lax.broadcasted_iota(jnp.int32, (rows, block_len), 1) < limits
    scores = jnp.where(visible, scores, HIDDEN)
    peak = jnp.max(scores, axis=1, keepdims=True)
    weights = jnp.where(visible, jnp.exp(scores - peak), 0.0)
    total = jnp.sum(weights, axis=1, keepdims=True)
    summed = jnp.dot(weights.astype(BF16), cache_ref[:, :latent], preferred_element_type=F32)
    out_ref[:, :latent] = summed.astype(BF16)
    lane = lax.broadcasted_iota(jnp.int32, (rows, 128), 1)
    stats = jnp.zeros((rows, 128), F32)
    for i, term in enumerate(split3(peak) + split3(total)):
        stats = jnp.where(lane == i, term, stats)
    out_ref[:, latent:] = stats.astype(BF16)


def combine_kernel(heads, tokens, latent, sums_ref, parts_ref, out_ref):
    stats = sums_ref[:, :, latent:].astype(F32)
    peak = stats[:, :, 0:1] + stats[:, :, 1:2] + stats[:, :, 2:3]
    total = stats[:, :, 3:4] + stats[:, :, 4:5] + stats[:, :, 5:6]
    top = jnp.max(peak, axis=0, keepdims=True)
    factor = jnp.exp(peak - top)
    total = jnp.sum(factor * total, axis=0)
    summed = jnp.sum(factor * sums_ref[:, :, :latent].astype(F32), axis=0)
    mixed = (summed / total).astype(BF16)
    groups, rows = parts_ref.shape[0], parts_ref.shape[1]
    depth = latent // groups
    first = rows - heads * depth
    values = jnp.concatenate(
        [
            parts_ref[:, first + h * depth : first + (h + 1) * depth, :].reshape(latent, 128)
            for h in range(heads)
        ],
        1,
    )
    out = jnp.dot(mixed, values, preferred_element_type=F32)
    for t in range(tokens):
        for h in range(heads):
            out_ref[0, t : t + 1, h * 128 : (h + 1) * 128] = out[
                t * heads + h : t * heads + h + 1, h * 128 : (h + 1) * 128
            ].astype(BF16)


def call(kernel, shape, count, specs=None):
    return pl.pallas_call(
        kernel,
        out_shape=jax.ShapeDtypeStruct(shape, BF16),
        in_specs=specs or [VMEM] * count,
        out_specs=VMEM,
        compiler_params=PARAMS,
    )


def body(groups, owners, query_nope, query_rope, latent_cache, lengths, key_up, value_up):
    heads, depth, latent = key_up.shape
    tokens = query_nope.shape[1]
    head_width = query_nope.shape[2] // heads
    rope_width = query_rope.shape[2] // heads
    per_owner = tokens * heads
    wide = latent + 128
    part_rows = (key_up.size + value_up.size) // 128
    copies = call(pack_kernel, (groups, part_rows, 128), 2)(key_up, value_up)
    parts = lax.all_to_all(copies, "batch", 0, 0, tiled=True)
    queries = call(
        functools.partial(absorb_kernel, heads, latent), (owners, per_owner, wide), 3
    )(parts, query_nope, query_rope)
    queries = lax.all_to_all(queries, "seq", 0, 0, tiled=True)
    scale = 1.0 / math.sqrt(head_width + rope_width)
    sums = call(
        functools.partial(attend_kernel, heads, tokens, scale, latent),
        (owners * per_owner, wide),
        3,
        [VMEM, VMEM, SMEM],
    )(queries.reshape(owners * per_owner, wide), latent_cache[0], lengths)
    sums = lax.all_to_all(sums.reshape(owners, per_owner, wide), "seq", 0, 0, tiled=True)
    return call(
        functools.partial(combine_kernel, heads, tokens, latent),
        (1, tokens, heads * 128),
        2,
    )(sums, parts)


def solution(mesh):
    in_specs = (
        P("batch", None, "seq"),
        P("batch", None, "seq"),
        P("batch", "seq", None),
        P("batch"),
        P("seq", "batch", None),
        P("seq", "batch", None),
    )
    out_specs = P("batch", None, "seq")
    run = functools.partial(body, mesh.shape["batch"], mesh.shape["seq"])
    return jax.shard_map(run, mesh=mesh, in_specs=in_specs, out_specs=out_specs, check_vma=False)
```

time: 534 us -> 92.1 us (0.17)
  the two profiles are of different devices: /device:TPU:2 before, /device:TPU:32 now
where the time goes in v1:
time: 92.1 us; the launch traced here: 91.7 us
  blocking collectives  44.4 us (48%)
  waiting for transfers between devices  22.6 us (25%)
  starting transfers between devices  18.4 us (20%)
  Pallas kernels  3.28 us (4%)
  local copies, waits for them, and re-layouts  2.41 us (3%)
    all_to_all x1, blocking collectives, body(): lax.all_to_all(sums.reshape(owners, per_owner, wide), 'seq', 0, 0, tiled=...  29.7 us
    all_to_all x1, waiting for transfers between devices, body(): queries = lax.all_to_all(queries, 'seq', 0, 0, tiled=True)  22.6 us
    all_to_all x1, starting transfers between devices, body(): queries = lax.all_to_all(queries, 'seq', 0, 0, tiled=True)  18.4 us
    all_to_all x1, blocking collectives, body(): parts = lax.all_to_all(copies, 'batch', 0, 0, tiled=True)  14.6 us
    unnamed x11, local copies, waits for them, and re-layouts  2.25 us
  transfers between devices with their start and end apart: 1, of which 1 were waited for; matrix products, arithmetic and copies ran while one was open for 1% of the time, Pallas kernels for 0%

profile of v1, /device:TPU:32, one launch (start us, length us, event | category | flops | bytes accessed | tf_op | source)
XLA Modules:
  0.0 91.7 jit_solution(16933793184226119602)
XLA Ops:
  0.0 0.0 copy-start
  0.0 0.8 copy-done
  0.8 0.0 copy-start.1
  0.8 0.8 copy-done.1
  1.5 0.0 copy-start.2
  1.5 0.0 copy-start.3
  1.5 0.1 shard_map.64
  1.6 0.0 copy-start.4
  1.6 14.6 %all_to_all.15.parts_ref = bf16[8,256,128]{2,1,0:T(8,128)(2,1)S(1)} all-to-all(bf16[8,256,128]{2,1,0:T(8,128)(2,1)S(1)} %shard_map.64), channel_id=1, replica_groups=mesh['batch'=8,'seq'=64] {'batch'}, dimensions={0} | all-to-all | bytes 1048576 | tf_op jit(solution)/shard_map/all_to_all | solution.py:150
  16.2 0.0 copy-done.2
  16.2 0.0 copy-done.3
  16.2 0.9 shard_map.65
  17.1 18.4 %all-to-all-start.1 = ((bf16[64,4,640]{2,1,0:T(4,128)(2,1)}), bf16[64,4,640]{2,1,0:T(4,128)(2,1)S(1)}, u32[]{:S(2)}, u32[]{:S(2)}) async-start(bf16[64,4,640]{2,1,0:T(4,128)(2,1)} %shard_map.65), calls=%async_computation.1 | async-start | bytes 655360 | tf_op jit(solution)/shard_map/all_to_all | solution.py:154
  36.2 0.0 copy-done.4
  36.2 0.7 copy.7
  36.9 22.6 %all-to-all-done.1 = bf16[64,4,640]{2,1,0:T(4,128)(2,1)S(1)} async-done(((bf16[64,4,640]{2,1,0:T(4,128)(2,1)}), bf16[64,4,640]{2,1,0:T(4,128)(2,1)S(1)}, u32[]{:S(2)}, u32[]{:S(2)}) %all-to-all-start.1) | async-done | bytes 327712 | tf_op jit(solution)/shard_map/all_to_all | solution.py:154
  59.5 0.1 reshape.6.query_ref
  59.6 1.2 %shard_map.66 = bf16[256,640]{1,0:T(8,128)(2,1)S(1)} custom-call(bf16[256,640]{1,0:T(8,128)(2,1)S(1)} %reshape.6.query_ref, bf16[1024,576]{1,0:T(8,128)(2,1)S(1)} %bitcast.1, s32[1]{0:T(128)S(6)} %copy.8.length_ref), custom_call_target="tpu_custom_call" | custom-call | tf_op jit(solution)/shard_map/pallas_call | solution.py:156
  60.8 0.1 reshape.7
  60.9 29.7 %all_to_all.16.sums_ref = bf16[64,4,640]{2,1,0:T(4,128)(2,1)S(1)} all-to-all(bf16[64,4,640]{2,1,0:T(4,128)(2,1)S(1)} %reshape.7), channel_id=1, replica_groups=mesh['batch'=8,'seq'=64] {'seq'}, dimensions={0} | all-to-all | bytes 655360 | tf_op jit(solution)/shard_map/all_to_all | solution.py:162
  90.7 1.1 %shard_map.67 = bf16[1,2,256]{2,1,0:T(2,128)(2,1)} custom-call(bf16[64,4,640]{2,1,0:T(4,128)(2,1)S(1)} %all_to_all.16.sums_ref, bf16[8,256,128]{2,1,0:T(8,128)(2,1)S(1)} %all_to_all.15.parts_ref), custom_call_target="tpu_custom_call" | custom-call | tf_op jit(solution)/shard_map/pallas_call | solution.py:163
Async XLA Ops:
  0.0 0.8 copy-start
  0.8 0.8 copy-start.1
  1.5 14.7 %copy-start.2 = (bf16[1,2,256]{2,1,0:T(2,128)(2,1)S(1)}, bf16[1,2,256]{2,1,0:T(2,128)(2,1)}, u32[]{:S(2)}) copy-start(bf16[1,2,256]{2,1,0:T(2,128)(2,1)} %nope_ref.1) | copy-start | bytes 3076
  1.5 14.7 %copy-start.3 = (bf16[1,2,128]{2,1,0:T(2,128)(2,1)S(1)}, bf16[1,2,128]{2,1,0:T(2,128)(2,1)}, u32[]{:S(2)}) copy-start(bf16[1,2,128]{2,1,0:T(2,128)(2,1)} %rope_ref.1) | copy-start | bytes 1540
  1.6 34.6 %copy-start.4 = (bf16[1,1024,576]{1,2,0:T(8,128)(2,1)S(1)}, bf16[1,1024,576]{1,2,0:T(8,128)(2,1)}, u32[]{:S(2)}) copy-start(bf16[1,1024,576]{1,2,0:T(8,128)(2,1)} %param.8) | copy-start | bytes 3538948
  17.1 42.4 %all-to-all-start.1 = ((bf16[64,4,640]{2,1,0:T(4,128)(2,1)}), bf16[64,4,640]{2,1,0:T(4,128)(2,1)S(1)}, u32[]{:S(2)}, u32[]{:S(2)}) async-start(bf16[64,4,640]{2,1,0:T(4,128)(2,1)} %shard_map.65), calls=%async_computation.1 | async-start | bytes 655360 | tf_op jit(solution)/shard_map/all_to_all | solution.py:154

commit v2 on v1

--- a/solution.py
+++ b/solution.py
@@ -6,6 +6,7 @@
 from jax import lax
 from jax.experimental import pallas as pl
 from jax.experimental.pallas import tpu as pltpu
+from jax.sharding import Mesh
 from jax.sharding import PartitionSpec as P
 
 VMEM = pl.BlockSpec(memory_space=pltpu.VMEM)
@@ -73,18 +74,43 @@
     out_ref[...] = jnp.broadcast_to(local[None], out_ref.shape).astype(BF16)
 
 
+def merge(blocks):
+    return jnp.concatenate([blocks[i] for i in range(blocks.shape[0])], 0)
+
+
+def spread_kernel(query_ref, out_ref):
+    rows = merge(query_ref[...].astype(F32)).astype(BF16)
+    for i in range(out_ref.shape[0]):
+        out_ref[i] = rows
+
+
+def with_stats(peak, total):
+    lane = lax.broadcasted_iota(jnp.int32, peak.shape[:-1] + (128,), peak.ndim - 1)
+    stats = jnp.zeros(lane.shape, F32)
+    for i, term in enumerate(split3(peak) + split3(total)):
+        stats = jnp.where(lane == i, term, stats)
+    return stats
+
+
+def combined(latent, sums_ref):
+    stats = sums_ref[:, :, latent:].astype(F32)
+    peak = stats[:, :, 0:1] + stats[:, :, 1:2] + stats[:, :, 2:3]
+    total = stats[:, :, 3:4] + stats[:, :, 4:5] + stats[:, :, 5:6]
+    top = jnp.max(peak, axis=0)
+    factor = jnp.exp(peak - top[None])
+    total = jnp.sum(factor * total, axis=0)
+    summed = jnp.sum(factor * sums_ref[:, :, :latent].astype(F32), axis=0)
+    return summed, top, total
+
+
 def attend_kernel(heads, tokens, scale, latent, query_ref, cache_ref, length_ref, out_ref):
     rows = query_ref.shape[0]
-    block_len, width = cache_ref.shape
-    contract = (((1,), (1,)), ((), ()))
-    scores = lax.dot_general(
-        query_ref[:, :latent], cache_ref[:, :latent], contract, preferred_element_type=F32
-    )
-    scores += lax.dot_general(
-        query_ref[:, latent:width], cache_ref[:, latent:width], contract, preferred_element_type=F32
-    )
+    width, block_len = cache_ref.shape
+    scores = jnp.dot(query_ref[:, :latent], cache_ref[:latent], preferred_element_type=F32)
+    scores += jnp.dot(query_ref[:, latent:width], cache_ref[latent:], preferred_element_type=F32)
     scores = scores * scale
-    limit = length_ref[0] - tokens + 1 - lax.axis_index("seq") * block_len
+    block = lax.axis_index("z") * lax.axis_size("y") + lax.axis_index("y")
+    limit = length_ref[0] - tokens + 1 - block * block_len
     row = lax.broadcasted_iota(jnp.int32, (rows, 1), 0)
     limits = limit + (row // heads) % tokens
     visible = lax.broadcasted_iota(jnp.int32, (rows, block_len), 1) < limits
@@ -92,23 +118,26 @@
     peak = jnp.max(scores, axis=1, keepdims=True)
     weights = jnp.where(visible, jnp.exp(scores - peak), 0.0)
     total = jnp.sum(weights, axis=1, keepdims=True)
-    summed = jnp.dot(weights.astype(BF16), cache_ref[:, :latent], preferred_element_type=F32)
+    summed = lax.dot_general(
+        weights.astype(BF16),
+        cache_ref[:latent],
+        (((1,), (1,)), ((), ())),
+        preferred_element_type=F32,
+    )
     out_ref[:, :latent] = summed.astype(BF16)
-    lane = lax.broadcasted_iota(jnp.int32, (rows, 128), 1)
-    stats = jnp.zeros((rows, 128), F32)
-    for i, term in enumerate(split3(peak) + split3(total)):
-        stats = jnp.where(lane == i, term, stats)
-    out_ref[:, latent:] = stats.astype(BF16)
+    out_ref[:, latent:] = with_stats(peak, total).astype(BF16)
+
+
+def add_kernel(latent, sums_ref, out_ref):
+    summed, top, total = combined(latent, sums_ref)
+    out = jnp.concatenate([summed, with_stats(top, total)], 1)
+    rows = out_ref.shape[1]
+    for i in range(out_ref.shape[0]):
+        out_ref[i] = out[i * rows : (i + 1) * rows].astype(BF16)
 
 
 def combine_kernel(heads, tokens, latent, sums_ref, parts_ref, out_ref):
-    stats = sums_ref[:, :, latent:].astype(F32)
-    peak = stats[:, :, 0:1] + stats[:, :, 1:2] + stats[:, :, 2:3]
-    total = stats[:, :, 3:4] + stats[:, :, 4:5] + stats[:, :, 5:6]
-    top = jnp.max(peak, axis=0, keepdims=True)
-    factor = jnp.exp(peak - top)
-    total = jnp.sum(factor * total, axis=0)
-    summed = jnp.sum(factor * sums_ref[:, :, :latent].astype(F32), axis=0)
+    summed, _, total = combined(latent, sums_ref)
     mixed = (summed / total).astype(BF16)
     groups, rows = parts_ref.shape[0], parts_ref.shape[1]
     depth = latent // groups
@@ -138,44 +167,49 @@
     )
 
 
-def body(groups, owners, query_nope, query_rope, latent_cache, lengths, key_up, value_up):
+def body(sizes, query_nope, query_rope, latent_cache, lengths, key_up, value_up):
     heads, depth, latent = key_up.shape
+    groups, high, low = sizes["batch"], sizes["z"], sizes["y"]
     tokens = query_nope.shape[1]
     head_width = query_nope.shape[2] // heads
     rope_width = query_rope.shape[2] // heads
-    per_owner = tokens * heads
+    own = tokens * heads
     wide = latent + 128
     part_rows = (key_up.size + value_up.size) // 128
     copies = call(pack_kernel, (groups, part_rows, 128), 2)(key_up, value_up)
     parts = lax.all_to_all(copies, "batch", 0, 0, tiled=True)
-    queries = call(
-        functools.partial(absorb_kernel, heads, latent), (owners, per_owner, wide), 3
-    )(parts, query_nope, query_rope)
-    queries = lax.all_to_all(queries, "seq", 0, 0, tiled=True)
+    absorb = functools.partial(absorb_kernel, heads, latent)
+    queries = call(absorb, (high, own, wide), 3)(parts, query_nope, query_rope)
+    queries = lax.all_to_all(queries, "z", 0, 0, tiled=True)
+    queries = call(spread_kernel, (low, high * own, wide), 1)(queries)
+    queries = lax.all_to_all(queries, "y", 0, 0, tiled=True)
     scale = 1.0 / math.sqrt(head_width + rope_width)
-    sums = call(
-        functools.partial(attend_kernel, heads, tokens, scale, latent),
-        (owners * per_owner, wide),
-        3,
-        [VMEM, VMEM, SMEM],
-    )(queries.reshape(owners * per_owner, wide), latent_cache[0], lengths)
-    sums = lax.all_to_all(sums.reshape(owners, per_owner, wide), "seq", 0, 0, tiled=True)
-    return call(
-        functools.partial(combine_kernel, heads, tokens, latent),
-        (1, tokens, heads * 128),
-        2,
-    )(sums, parts)
+    attend = functools.partial(attend_kernel, heads, tokens, scale, latent)
+    sums = call(attend, (low * high * own, wide), 3, [VMEM, VMEM, SMEM])(
+        queries.reshape(low * high * own, wide), latent_cache[0].T, lengths
+    )
+    sums = lax.all_to_all(sums.reshape(low, high * own, wide), "y", 0, 0, tiled=True)
+    sums = call(functools.partial(add_kernel, latent), (high, own, wide), 1)(sums)
+    sums = lax.all_to_all(sums, "z", 0, 0, tiled=True)
+    combine = functools.partial(combine_kernel, heads, tokens, latent)
+    return call(combine, (1, tokens, heads * 128), 2)(sums, parts)
+
+
+Y_SIZE = 4
 
 
 def solution(mesh):
+    batch, seq = mesh.shape["batch"], mesh.shape["seq"]
+    mesh = Mesh(mesh.devices.reshape(batch, seq // Y_SIZE, Y_SIZE), ("batch", "z", "y"))
+    both = ("z", "y")
     in_specs = (
-        P("batch", None, "seq"),
-        P("batch", None, "seq"),
-        P("batch", "seq", None),
+        P("batch", None, both),
+        P("batch", None, both),
+        P("batch", both, None),
         P("batch"),
-        P("seq", "batch", None),
-        P("seq", "batch", None),
-    )
-    out_specs = P("batch", None, "seq")
-    run = functools.partial(body, mesh.shape["batch"], mesh.shape["seq"])
+        P(both, "batch", None),
+        P(both, "batch", None),
+    )
+    out_specs = P("batch", None, both)
+    run = functools.partial(body, dict(mesh.shape))
     return jax.shard_map(run, mesh=mesh, in_specs=in_specs, out_specs=out_specs, check_vma=False)

time: 92.1 us -> 84 us (0.912)
  blocking collectives: 44.4 us -> 67.1 us
  waiting for transfers between devices: 22.6 us -> 6.38 us
  starting transfers between devices: 18.4 us -> 4.46 us
    all_to_all x1 -> x3, blocking collectives: 29.7 us -> 52.6 us  [the longest x1 26.9 us: body(): queries = lax.all_to_all(queries, 'z', 0, 0, tiled=True)]
    all_to_all x1, waiting for transfers between devices: 22.6 us -> 6.38 us  [body(): queries = lax.all_to_all(queries, 'y', 0, 0, tiled=True)]
    all_to_all x1, starting transfers between devices: 18.4 us -> 4.46 us  [body(): queries = lax.all_to_all(queries, 'y', 0, 0, tiled=True)]
    unnamed x11 -> x10, local copies, waits for them, and re-layouts: 2.25 us -> 1.53 us
    pallas_call x3 -> x5, Pallas kernels: 3.21 us -> 3.35 us  [the longest x1 1.22 us: body(): call(attend, (low * high * own, wide), 3, [VMEM, VMEM, SMEM])]
  transfers between devices with their start and end apart: 1 -> 1, of which waited for: 1 -> 1; matrix products, arithmetic and copies ran while one was open for 1% -> 0% of each run, Pallas kernels for 0% -> 0%
where the time goes in v2:
time: 84 us; the launch traced here: 83.5 us
  blocking collectives  67.1 us (80%)
  waiting for transfers between devices  6.38 us (8%)
  starting transfers between devices  4.46 us (5%)
  Pallas kernels  3.42 us (4%)
  local copies, waits for them, and re-layouts  1.53 us (2%)
    all_to_all x1, blocking collectives, body(): queries = lax.all_to_all(queries, 'z', 0, 0, tiled=True)  26.9 us
    all_to_all x1, blocking collectives, body(): sums = lax.all_to_all(sums, 'z', 0, 0, tiled=True)  16.3 us
    all_to_all x1, blocking collectives, body(): parts = lax.all_to_all(copies, 'batch', 0, 0, tiled=True)  14.5 us
    all_to_all x1, blocking collectives, body(): lax.all_to_all(sums.reshape(low, high * own, wide), 'y', 0, 0, tiled=True)  9.4 us
    all_to_all x1, waiting for transfers between devices, body(): queries = lax.all_to_all(queries, 'y', 0, 0, tiled=True)  6.38 us
    all_to_all x1, starting transfers between devices, body(): queries = lax.all_to_all(queries, 'y', 0, 0, tiled=True)  4.46 us
  transfers between devices with their start and end apart: 1, of which 1 were waited for; matrix products, arithmetic and copies ran while one was open for 0% of the time, Pallas kernels for 0%

profile of v2, /device:TPU:32, one launch (start us, length us, event | category | flops | bytes accessed | tf_op | source)
XLA Modules:
  0.0 83.5 jit_solution(6070278525976577469)
XLA Ops:
  0.0 0.0 copy-start.1
  0.0 0.8 copy-done.1
  0.8 0.0 copy-start.2
  0.8 0.8 copy-done.2
  1.5 0.0 copy-start.3
  1.5 0.0 copy-start.4
  1.5 0.1 shard_map.64
  1.6 14.5 %all_to_all.25.parts_ref = bf16[8,256,128]{2,1,0:T(8,128)(2,1)S(1)} all-to-all(bf16[8,256,128]{2,1,0:T(8,128)(2,1)S(1)} %shard_map.64), channel_id=1, replica_groups=mesh['batch'=8,'z'=16,'y'=4] {'batch'}, dimensions={0} | all-to-all | bytes 1048576 | tf_op jit(solution)/shard_map/all_to_all | solution.py:180
  16.1 0.0 copy-done.3
  16.1 0.0 copy-done.4
  16.1 0.0 copy-start
  16.1 0.2 shard_map.65
  16.2 26.9 %all_to_all.26.query_ref = bf16[16,4,640]{2,1,0:T(4,128)(2,1)S(1)} all-to-all(bf16[16,4,640]{2,1,0:T(4,128)(2,1)S(1)} %shard_map.65), channel_id=1, replica_groups=mesh['batch'=8,'z'=16,'y'=4] {'z'}, dimensions={0} | all-to-all | bytes 163840 | tf_op jit(solution)/shard_map/all_to_all | solution.py:183
  43.1 0.8 shard_map.66
  43.9 4.5 %all-to-all-start.2 = ((bf16[4,64,640]{2,1,0:T(8,128)(2,1)}), bf16[4,64,640]{2,1,0:T(8,128)(2,1)S(1)}, u32[]{:S(2)}, u32[]{:S(2)}) async-start(bf16[4,64,640]{2,1,0:T(8,128)(2,1)} %shard_map.66), calls=%async_computation.2 | async-start | bytes 655360 | tf_op jit(solution)/shard_map/all_to_all | solution.py:185
  49.0 6.4 %all-to-all-done.2 = bf16[4,64,640]{2,1,0:T(8,128)(2,1)S(1)} async-done(((bf16[4,64,640]{2,1,0:T(8,128)(2,1)}), bf16[4,64,640]{2,1,0:T(8,128)(2,1)S(1)}, u32[]{:S(2)}, u32[]{:S(2)}) %all-to-all-start.2) | async-done | bytes 327712 | tf_op jit(solution)/shard_map/all_to_all | solution.py:185
  55.4 0.0 copy-done
  55.4 1.2 %shard_map.67 = bf16[256,640]{1,0:T(8,128)(2,1)S(1)} custom-call(bf16[256,640]{1,0:T(8,128)(2,1)S(1)} %bitcast.5, bf16[576,1024]{1,0:T(8,128)(2,1)S(1)} %bitcast.7, s32[1]{0:T(128)S(6)} %copy.7.length_ref), custom_call_target="tpu_custom_call" | custom-call | tf_op jit(solution)/shard_map/pallas_call | solution.py:188
  56.6 9.4 %all_to_all.27.sums_ref = bf16[4,64,640]{2,1,0:T(8,128)(2,1)S(1)} all-to-all(bf16[4,64,640]{2,1,0:T(8,128)(2,1)S(1)} %bitcast.6), channel_id=1, replica_groups=mesh['batch'=8,'z'=16,'y'=4] {'y'}, dimensions={0} | all-to-all | bytes 655360 | tf_op jit(solution)/shard_map/all_to_all | solution.py:191
  66.0 0.3 shard_map.68
  66.3 16.3 %all_to_all.28.sums_ref = bf16[16,4,640]{2,1,0:T(4,128)(2,1)S(1)} all-to-all(bf16[16,4,640]{2,1,0:T(4,128)(2,1)S(1)} %shard_map.68), channel_id=1, replica_groups=mesh['batch'=8,'z'=16,'y'=4] {'z'}, dimensions={0} | all-to-all | bytes 163840 | tf_op jit(solution)/shard_map/all_to_all | solution.py:193
  82.6 0.9 %shard_map.69 = bf16[1,2,256]{2,1,0:T(2,128)(2,1)} custom-call(bf16[16,4,640]{2,1,0:T(4,128)(2,1)S(1)} %all_to_all.28.sums_ref, bf16[8,256,128]{2,1,0:T(8,128)(2,1)S(1)} %all_to_all.25.parts_ref), custom_call_target="tpu_custom_call" | custom-call | tf_op jit(solution)/shard_map/pallas_call | solution.py:195
Async XLA Ops:
  0.0 0.8 copy-start.1
  0.8 0.8 copy-start.2
  1.5 14.6 %copy-start.3 = (bf16[1,2,256]{2,1,0:T(2,128)(2,1)S(1)}, bf16[1,2,256]{2,1,0:T(2,128)(2,1)}, u32[]{:S(2)}) copy-start(bf16[1,2,256]{2,1,0:T(2,128)(2,1)} %nope_ref.1) | copy-start | bytes 3076
  1.5 14.6 %copy-start.4 = (bf16[1,2,128]{2,1,0:T(2,128)(2,1)S(1)}, bf16[1,2,128]{2,1,0:T(2,128)(2,1)}, u32[]{:S(2)}) copy-start(bf16[1,2,128]{2,1,0:T(2,128)(2,1)} %rope_ref.1) | copy-start | bytes 1540
  16.1 39.3 %copy-start = (bf16[1,1024,576]{1,2,0:T(8,128)(2,1)S(1)}, bf16[1,1024,576]{1,2,0:T(8,128)(2,1)}, u32[]{:S(2)}) copy-start(bf16[1,1024,576]{1,2,0:T(8,128)(2,1)} %param.8) | copy-start | bytes 3538948
  43.9 11.5 %all-to-all-start.2 = ((bf16[4,64,640]{2,1,0:T(8,128)(2,1)}), bf16[4,64,640]{2,1,0:T(8,128)(2,1)S(1)}, u32[]{:S(2)}, u32[]{:S(2)}) async-start(bf16[4,64,640]{2,1,0:T(8,128)(2,1)} %shard_map.66), calls=%async_computation.2 | async-start | bytes 655360 | tf_op jit(solution)/shard_map/all_to_all | solution.py:185

commit v3 on v2

--- a/solution.py
+++ b/solution.py
@@ -10,11 +10,11 @@
 from jax.sharding import PartitionSpec as P
 
 VMEM = pl.BlockSpec(memory_space=pltpu.VMEM)
-SMEM = pl.BlockSpec(memory_space=pltpu.SMEM)
 PARAMS = pltpu.CompilerParams(vmem_limit_bytes=24 * 1024 * 1024)
 F32 = jnp.float32
 BF16 = jnp.bfloat16
 HIDDEN = -1e30
+LOG2_E = math.log2(math.e)
 
 
 def split3(x):
@@ -24,13 +24,26 @@
     return high, mid, (rest - mid).astype(BF16).astype(F32)
 
 
-def pack_kernel(key_ref, value_ref, out_ref):
-    heads, depth, latent = key_ref.shape
-    key = jnp.concatenate(
-        [key_ref[:, :, c : c + 128].reshape(heads * depth, 128) for c in range(0, latent, 128)], 0
-    )
-    value = value_ref[...].reshape(-1, 128)
-    both = jnp.concatenate([key, value], 0)
+def pack_kernel(
+    key_ref, value_ref, nope_ref, rope_ref, out_ref, nope_out, rope_out, key, value, sems
+):
+    pairs = (
+        (key_ref, key),
+        (value_ref, value),
+        (nope_ref, nope_out),
+        (rope_ref, rope_out),
+    )
+    copies = [
+        pltpu.make_async_copy(source, target, sems.at[i])
+        for i, (source, target) in enumerate(pairs)
+    ]
+    for copy in copies:
+        copy.start()
+    for copy in copies:
+        copy.wait()
+    heads, depth, latent = key.shape
+    rows = [key[:, :, c : c + 128].reshape(heads * depth, 128) for c in range(0, latent, 128)]
+    both = jnp.concatenate(rows + [value[...].reshape(-1, 128)], 0)
     for i in range(out_ref.shape[0]):
         out_ref[i] = both
 
@@ -74,16 +87,6 @@
     out_ref[...] = jnp.broadcast_to(local[None], out_ref.shape).astype(BF16)
 
 
-def merge(blocks):
-    return jnp.concatenate([blocks[i] for i in range(blocks.shape[0])], 0)
-
-
-def spread_kernel(query_ref, out_ref):
-    rows = merge(query_ref[...].astype(F32)).astype(BF16)
-    for i in range(out_ref.shape[0]):
-        out_ref[i] = rows
-
-
 def with_stats(peak, total):
     lane = lax.broadcasted_iota(jnp.int32, peak.shape[:-1] + (128,), peak.ndim - 1)
     stats = jnp.zeros(lane.shape, F32)
@@ -108,16 +111,16 @@
     width, block_len = cache_ref.shape
     scores = jnp.dot(query_ref[:, :latent], cache_ref[:latent], preferred_element_type=F32)
     scores += jnp.dot(query_ref[:, latent:width], cache_ref[latent:], preferred_element_type=F32)
-    scores = scores * scale
     block = lax.axis_index("z") * lax.axis_size("y") + lax.axis_index("y")
     limit = length_ref[0] - tokens + 1 - block * block_len
     row = lax.broadcasted_iota(jnp.int32, (rows, 1), 0)
     limits = limit + (row // heads) % tokens
     visible = lax.broadcasted_iota(jnp.int32, (rows, block_len), 1) < limits
     scores = jnp.where(visible, scores, HIDDEN)
-    peak = jnp.max(scores, axis=1, keepdims=True)
-    weights = jnp.where(visible, jnp.exp(scores - peak), 0.0)
+    peak = jnp.maximum(jnp.max(scores, axis=1, keepdims=True), HIDDEN / 2)
+    weights = jnp.exp2((scores - peak) * (scale * LOG2_E))
     total = jnp.sum(weights, axis=1, keepdims=True)
+    peak = peak * scale
     summed = lax.dot_general(
         weights.astype(BF16),
         cache_ref[:latent],
@@ -176,16 +179,35 @@
     own = tokens * heads
     wide = latent + 128
     part_rows = (key_up.size + value_up.size) // 128
-    copies = call(pack_kernel, (groups, part_rows, 128), 2)(key_up, value_up)
+    like = jax.ShapeDtypeStruct
+    copies, nope, rope = pl.pallas_call(
+        pack_kernel,
+        out_shape=(
+            like((groups, part_rows, 128), BF16),
+            like(query_nope.shape, BF16),
+            like(query_rope.shape, BF16),
+        ),
+        in_specs=[pl.BlockSpec(memory_space=pl.ANY)] * 4,
+        out_specs=[VMEM] * 3,
+        scratch_shapes=[
+            pltpu.VMEM(key_up.shape, BF16),
+            pltpu.VMEM(value_up.shape, BF16),
+            pltpu.SemaphoreType.DMA((4,)),
+        ],
+        compiler_params=PARAMS,
+    )(*[
+        pltpu.with_memory_space_constraint(array, pltpu.HBM)
+        for array in (key_up, value_up, query_nope, query_rope)
+    ])
     parts = lax.all_to_all(copies, "batch", 0, 0, tiled=True)
     absorb = functools.partial(absorb_kernel, heads, latent)
-    queries = call(absorb, (high, own, wide), 3)(parts, query_nope, query_rope)
+    queries = call(absorb, (high, own, wide), 3)(parts, nope, rope)
     queries = lax.all_to_all(queries, "z", 0, 0, tiled=True)
-    queries = call(spread_kernel, (low, high * own, wide), 1)(queries)
+    queries = jnp.broadcast_to(queries.reshape(high * own, wide), (low, high * own, wide))
     queries = lax.all_to_all(queries, "y", 0, 0, tiled=True)
     scale = 1.0 / math.sqrt(head_width + rope_width)
     attend = functools.partial(attend_kernel, heads, tokens, scale, latent)
-    sums = call(attend, (low * high * own, wide), 3, [VMEM, VMEM, SMEM])(
+    sums = call(attend, (low * high * own, wide), 3, [VMEM, VMEM, pl.BlockSpec(memory_space=pltpu.SMEM)])(
         queries.reshape(low * high * own, wide), latent_cache[0].T, lengths
     )
     sums = lax.all_to_all(sums.reshape(low, high * own, wide), "y", 0, 0, tiled=True)

time: 84 us -> 83.1 us (0.989)
    unnamed x10 -> x2, local copies, waits for them, and re-layouts: 1.53 us -> 0.01 us
    pallas_call x4 -> x3, Pallas kernels: 2.21 us -> 2.12 us  [the longest x1 1.09 us: body(): call(attend, (low * high * own, wide), 3, [VMEM, VMEM, pl.BlockSpec(memor...]
where the time goes in v3:
time: 83.1 us; the launch traced here: 82.7 us
  blocking collectives  67 us (81%)
  waiting for transfers between devices  6.38 us (8%)
  starting transfers between devices  4.46 us (5%)
  Pallas kernels  3.32 us (4%)
    all_to_all x1, blocking collectives, body(): queries = lax.all_to_all(queries, 'z', 0, 0, tiled=True)  26.9 us
    all_to_all x1, blocking collectives, body(): sums = lax.all_to_all(sums, 'z', 0, 0, tiled=True)  16.3 us
    all_to_all x1, blocking collectives, body(): parts = lax.all_to_all(copies, 'batch', 0, 0, tiled=True)  14.5 us
    all_to_all x1, blocking collectives, body(): lax.all_to_all(sums.reshape(low, high * own, wide), 'y', 0, 0, tiled=True)  9.4 us
    all_to_all x1, waiting for transfers between devices, body(): queries = lax.all_to_all(queries, 'y', 0, 0, tiled=True)  6.38 us
    all_to_all x1, starting transfers between devices, body(): queries = lax.all_to_all(queries, 'y', 0, 0, tiled=True)  4.46 us
  transfers between devices with their start and end apart: 1, of which 1 were waited for; matrix products, arithmetic and copies ran while one was open for 0% of the time, Pallas kernels for 0%

profile of v3, /device:TPU:32, one launch (start us, length us, event | category | flops | bytes accessed | tf_op | source)
XLA Modules:
  0.0 82.7 jit_solution(11221404998109485228)
XLA Ops:
  0.0 0.9 %shard_map.64 = (bf16[8,256,128]{2,1,0:T(8,128)(2,1)S(1)}, bf16[1,2,256]{2,1,0:T(2,128)(2,1)S(1)}, bf16[1,2,128]{2,1,0:T(2,128)(2,1)S(1)}) custom-call(bf16[2,16,512]{2,1,0:T(8,128)(2,1)} %key_ref.1, bf16[2,64,128]{2,1,0:T(8,128)(2,1)} %value_ref.1, bf16[1,2,256]{2,1,0:T(2,128)(2,1)} %nope_ref.1, bf16[1,2,128]{2,1,0:T(2,128)(2,1)} %rope_ref.1), custom_call_target="tpu_custom_call" | custom-call | tf_op jit(solution)/shard_map/pallas_call | solution.py:183
  0.9 14.5 %all_to_all.25.parts_ref = bf16[8,256,128]{2,1,0:T(8,128)(2,1)S(1)} all-to-all(bf16[8,256,128]{2,1,0:T(8,128)(2,1)S(1)} %get-tuple-element.8), channel_id=1, replica_groups=mesh['batch'=8,'z'=16,'y'=4] {'batch'}, dimensions={0} | all-to-all | bytes 1048576 | tf_op jit(solution)/shard_map/all_to_all | solution.py:202
  15.4 0.0 copy-start
  15.4 0.2 shard_map.65
  15.5 26.9 %all_to_all.26 = bf16[16,4,640]{2,1,0:T(4,128)(2,1)S(1)} all-to-all(bf16[16,4,640]{2,1,0:T(4,128)(2,1)S(1)} %shard_map.65), channel_id=1, replica_groups=mesh['batch'=8,'z'=16,'y'=4] {'z'}, dimensions={0} | all-to-all | bytes 163840 | tf_op jit(solution)/shard_map/all_to_all | solution.py:205
  42.4 0.7 broadcast_in_dim.3
  43.2 4.5 %all-to-all-start.2 = ((bf16[4,64,640]{2,1,0:T(8,128)(2,1)}), bf16[4,64,640]{2,1,0:T(8,128)(2,1)S(1)}, u32[]{:S(2)}, u32[]{:S(2)}) async-start(bf16[4,64,640]{2,1,0:T(8,128)(2,1)} %broadcast_in_dim.3), calls=%async_computation.2 | async-start | bytes 655360 | tf_op jit(solution)/shard_map/all_to_all | solution.py:207
  48.3 6.4 %all-to-all-done.2 = bf16[4,64,640]{2,1,0:T(8,128)(2,1)S(1)} async-done(((bf16[4,64,640]{2,1,0:T(8,128)(2,1)}), bf16[4,64,640]{2,1,0:T(8,128)(2,1)S(1)}, u32[]{:S(2)}, u32[]{:S(2)}) %all-to-all-start.2) | async-done | bytes 327712 | tf_op jit(solution)/shard_map/all_to_all | solution.py:207
  54.7 0.0 copy-done
  54.7 1.1 %shard_map.66 = bf16[256,640]{1,0:T(8,128)(2,1)S(1)} custom-call(bf16[256,640]{1,0:T(8,128)(2,1)S(1)} %bitcast.5, bf16[576,1024]{1,0:T(8,128)(2,1)S(1)} %bitcast.7, s32[1]{0:T(128)S(6)} %copy.7.length_ref), custom_call_target="tpu_custom_call" | custom-call | tf_op jit(solution)/shard_map/pallas_call | solution.py:210
  55.8 9.4 %all_to_all.27.sums_ref = bf16[4,64,640]{2,1,0:T(8,128)(2,1)S(1)} all-to-all(bf16[4,64,640]{2,1,0:T(8,128)(2,1)S(1)} %bitcast.6), channel_id=1, replica_groups=mesh['batch'=8,'z'=16,'y'=4] {'y'}, dimensions={0} | all-to-all | bytes 655360 | tf_op jit(solution)/shard_map/all_to_all | solution.py:213
  65.2 0.3 shard_map.67
  65.5 16.3 %all_to_all.28.sums_ref = bf16[16,4,640]{2,1,0:T(4,128)(2,1)S(1)} all-to-all(bf16[16,4,640]{2,1,0:T(4,128)(2,1)S(1)} %shard_map.67), channel_id=1, replica_groups=mesh['batch'=8,'z'=16,'y'=4] {'z'}, dimensions={0} | all-to-all | bytes 163840 | tf_op jit(solution)/shard_map/all_to_all | solution.py:215
  81.7 0.9 %shard_map.68 = bf16[1,2,256]{2,1,0:T(2,128)(2,1)} custom-call(bf16[16,4,640]{2,1,0:T(4,128)(2,1)S(1)} %all_to_all.28.sums_ref, bf16[8,256,128]{2,1,0:T(8,128)(2,1)S(1)} %all_to_all.25.parts_ref), custom_call_target="tpu_custom_call" | custom-call | tf_op jit(solution)/shard_map/pallas_call | solution.py:217
  (1 shorter events, 0.0 us)
Async XLA Ops:
  15.4 39.3 %copy-start = (bf16[1,1024,576]{1,2,0:T(8,128)(2,1)S(1)}, bf16[1,1024,576]{1,2,0:T(8,128)(2,1)}, u32[]{:S(2)}) copy-start(bf16[1,1024,576]{1,2,0:T(8,128)(2,1)} %param.8) | copy-start | bytes 3538948
  43.2 11.5 %all-to-all-start.2 = ((bf16[4,64,640]{2,1,0:T(8,128)(2,1)}), bf16[4,64,640]{2,1,0:T(8,128)(2,1)S(1)}, u32[]{:S(2)}, u32[]{:S(2)}) async-start(bf16[4,64,640]{2,1,0:T(8,128)(2,1)} %broadcast_in_dim.3), calls=%async_computation.2 | async-start | bytes 655360 | tf_op jit(solution)/shard_map/all_to_all | solution.py:207

commit v4 on v3

--- a/solution.py
+++ b/solution.py
@@ -22,6 +22,10 @@
     rest = x - high
     mid = rest.astype(BF16).astype(F32)
     return high, mid, (rest - mid).astype(BF16).astype(F32)
+
+
+def places(groups):
+    return [(i - FIRST["batch"]) % groups for i in range(groups)]
 
 
 def pack_kernel(
@@ -57,10 +61,9 @@
     blocks = []
     for c in range(latent // 128):
         rows = [
-            parts_ref[:, (c * heads + h) * depth : (c * heads + h + 1) * depth, :].reshape(
-                head_width, 128
-            )
+            parts_ref[place, (c * heads + h) * depth : (c * heads + h + 1) * depth]
             for h in range(heads)
+            for place in places(groups)
         ]
         blocks.append(jnp.concatenate(rows, 0))
     keys = jnp.concatenate(blocks, 1)
@@ -147,7 +150,13 @@
     first = rows - heads * depth
     values = jnp.concatenate(
         [
-            parts_ref[:, first + h * depth : first + (h + 1) * depth, :].reshape(latent, 128)
+            jnp.concatenate(
+                [
+                    parts_ref[place, first + h * depth : first + (h + 1) * depth]
+                    for place in places(groups)
+                ],
+                0,
+            )
             for h in range(heads)
         ],
         1,
@@ -168,6 +177,18 @@
         out_specs=VMEM,
         compiler_params=PARAMS,
     )
+
+
+FIRST = {"batch": 5, "z": 8, "y": 2}
+
+
+def order(axis, size):
+    return [(i + FIRST[axis]) % size for i in range(size)]
+
+
+def exchange(blocks, axis):
+    groups = [order(axis, blocks.shape[0])]
+    return lax.all_to_all(blocks, axis, 0, 0, axis_index_groups=groups, tiled=True)
 
 
 def body(sizes, query_nope, query_rope, latent_cache, lengths, key_up, value_up):
@@ -199,20 +220,20 @@
         pltpu.with_memory_space_constraint(array, pltpu.HBM)
         for array in (key_up, value_up, query_nope, query_rope)
     ])
-    parts = lax.all_to_all(copies, "batch", 0, 0, tiled=True)
+    parts = exchange(copies, "batch")
     absorb = functools.partial(absorb_kernel, heads, latent)
     queries = call(absorb, (high, own, wide), 3)(parts, nope, rope)
-    queries = lax.all_to_all(queries, "z", 0, 0, tiled=True)
+    queries = exchange(queries, "z")
     queries = jnp.broadcast_to(queries.reshape(high * own, wide), (low, high * own, wide))
-    queries = lax.all_to_all(queries, "y", 0, 0, tiled=True)
+    queries = exchange(queries, "y")
     scale = 1.0 / math.sqrt(head_width + rope_width)
     attend = functools.partial(attend_kernel, heads, tokens, scale, latent)
     sums = call(attend, (low * high * own, wide), 3, [VMEM, VMEM, pl.BlockSpec(memory_space=pltpu.SMEM)])(
         queries.reshape(low * high * own, wide), latent_cache[0].T, lengths
     )
-    sums = lax.all_to_all(sums.reshape(low, high * own, wide), "y", 0, 0, tiled=True)
+    sums = exchange(sums.reshape(low, high * own, wide), "y")
     sums = call(functools.partial(add_kernel, latent), (high, own, wide), 1)(sums)
-    sums = lax.all_to_all(sums, "z", 0, 0, tiled=True)
+    sums = exchange(sums, "z")
     combine = functools.partial(combine_kernel, heads, tokens, latent)
     return call(combine, (1, tokens, heads * 128), 2)(sums, parts)
 

time: 83.1 us -> 75.5 us (0.909)
  the two profiles are of different devices: /device:TPU:32 before, /device:TPU:4 now
where the time goes in v4:
time: 75.5 us; the launch traced here: 75.1 us
  blocking collectives  60.3 us (80%)
  starting transfers between devices  6.62 us (9%)
  waiting for transfers between devices  3.41 us (5%)
  Pallas kernels  3.32 us (4%)
  local copies, waits for them, and re-layouts  0.77 us (1%)
    all_to_all x4, blocking collectives, exchange(): lax.all_to_all(blocks, axis, 0, 0, axis_index_groups=groups, tiled=True)  60.3 us
    all_to_all x1, starting transfers between devices, exchange(): lax.all_to_all(blocks, axis, 0, 0, axis_index_groups=groups, tiled=True)  6.62 us
    all_to_all x1, waiting for transfers between devices, exchange(): lax.all_to_all(blocks, axis, 0, 0, axis_index_groups=groups, tiled=True)  3.41 us
  transfers between devices with their start and end apart: 1, of which 1 were waited for; matrix products, arithmetic and copies ran while one was open for 0% of the time, Pallas kernels for 0%

profile of v4, /device:TPU:4, one launch (start us, length us, event | category | flops | bytes accessed | tf_op | source)
XLA Modules:
  0.0 75.1 jit_solution(10432220014725164234)
XLA Ops:
  0.0 0.9 %shard_map.64 = (bf16[8,256,128]{2,1,0:T(8,128)(2,1)S(1)}, bf16[1,2,256]{2,1,0:T(2,128)(2,1)S(1)}, bf16[1,2,128]{2,1,0:T(2,128)(2,1)S(1)}) custom-call(bf16[2,16,512]{2,1,0:T(8,128)(2,1)} %key_ref.1, bf16[2,64,128]{2,1,0:T(8,128)(2,1)} %value_ref.1, bf16[1,2,256]{2,1,0:T(2,128)(2,1)} %nope_ref.1, bf16[1,2,128]{2,1,0:T(2,128)(2,1)} %rope_ref.1), custom_call_target="tpu_custom_call" | custom-call | tf_op jit(solution)/shard_map/pallas_call | solution.py:204
  0.9 17.0 %all_to_all.25.parts_ref = bf16[8,256,128]{2,1,0:T(8,128)(2,1)S(1)} all-to-all(bf16[8,256,128]{2,1,0:T(8,128)(2,1)S(1)} %get-tuple-element.8), channel_id=1, replica_groups={{320,384,448,0,64,128,192,256},{321,385,449,1,65,129,193,257},{322,386,..., dimensions={0} | all-to-all | bytes 1048576 | tf_op jit(solution)/shard_map/all_to_all | solution.py:191
  17.9 0.0 copy-start
  17.9 0.2 shard_map.65
  18.1 18.1 %all_to_all.26 = bf16[16,4,640]{2,1,0:T(4,128)(2,1)S(1)} all-to-all(bf16[16,4,640]{2,1,0:T(4,128)(2,1)S(1)} %shard_map.65), channel_id=1, replica_groups={{32,36,40,44,48,52,56,60,0,4,8,12,16,20,24,28},{33,37,41,45,49,53,57,61..., dimensions={0} | all-to-all | bytes 163840 | tf_op jit(solution)/shard_map/all_to_all | solution.py:191
  36.2 0.7 broadcast_in_dim.3
  37.0 6.6 %all-to-all-start.2 = ((bf16[4,64,640]{2,1,0:T(8,128)(2,1)}), bf16[4,64,640]{2,1,0:T(8,128)(2,1)S(1)}, u32[]{:S(2)}, u32[]{:S(2)}) async-start(bf16[4,64,640]{2,1,0:T(8,128)(2,1)} %broadcast_in_dim.3), calls=%async_computation.2 | async-start | bytes 655360 | tf_op jit(solution)/shard_map/all_to_all | solution.py:191
  44.3 3.4 %all-to-all-done.2 = bf16[4,64,640]{2,1,0:T(8,128)(2,1)S(1)} async-done(((bf16[4,64,640]{2,1,0:T(8,128)(2,1)}), bf16[4,64,640]{2,1,0:T(8,128)(2,1)S(1)}, u32[]{:S(2)}, u32[]{:S(2)}) %all-to-all-start.2) | async-done | bytes 327712 | tf_op jit(solution)/shard_map/all_to_all | solution.py:191
  47.7 0.0 copy-done
  47.7 1.1 %shard_map.66 = bf16[256,640]{1,0:T(8,128)(2,1)S(1)} custom-call(bf16[256,640]{1,0:T(8,128)(2,1)S(1)} %bitcast.5, bf16[576,1024]{1,0:T(8,128)(2,1)S(1)} %bitcast.7, s32[1]{0:T(128)S(6)} %copy.7.length_ref), custom_call_target="tpu_custom_call" | custom-call | tf_op jit(solution)/shard_map/pallas_call | solution.py:231
  48.8 9.2 %all_to_all.27.sums_ref = bf16[4,64,640]{2,1,0:T(8,128)(2,1)S(1)} all-to-all(bf16[4,64,640]{2,1,0:T(8,128)(2,1)S(1)} %bitcast.6), channel_id=1, replica_groups={{2,3,0,1},{6,7,4,5},{10,11,8,9},{14,15,12,13},{18,19,16,17},{22,23,20,2..., dimensions={0} | all-to-all | bytes 655360 | tf_op jit(solution)/shard_map/all_to_all | solution.py:191
  58.0 0.3 shard_map.67
  58.3 15.9 %all_to_all.28.sums_ref = bf16[16,4,640]{2,1,0:T(4,128)(2,1)S(1)} all-to-all(bf16[16,4,640]{2,1,0:T(4,128)(2,1)S(1)} %shard_map.67), channel_id=1, replica_groups={{32,36,40,44,48,52,56,60,0,4,8,12,16,20,24,28},{33,37,41,45,49,53,57,61..., dimensions={0} | all-to-all | bytes 163840 | tf_op jit(solution)/shard_map/all_to_all | solution.py:191
  74.2 0.9 %shard_map.68 = bf16[1,2,256]{2,1,0:T(2,128)(2,1)} custom-call(bf16[16,4,640]{2,1,0:T(4,128)(2,1)S(1)} %all_to_all.28.sums_ref, bf16[8,256,128]{2,1,0:T(8,128)(2,1)S(1)} %all_to_all.25.parts_ref), custom_call_target="tpu_custom_call" | custom-call | tf_op jit(solution)/shard_map/pallas_call | solution.py:238
  (1 shorter events, 0.0 us)
Async XLA Ops:
  17.9 29.8 %copy-start = (bf16[1,1024,576]{1,2,0:T(8,128)(2,1)S(1)}, bf16[1,1024,576]{1,2,0:T(8,128)(2,1)}, u32[]{:S(2)}) copy-start(bf16[1,1024,576]{1,2,0:T(8,128)(2,1)} %param.8) | copy-start | bytes 3538948
  37.0 10.7 %all-to-all-start.2 = ((bf16[4,64,640]{2,1,0:T(8,128)(2,1)}), bf16[4,64,640]{2,1,0:T(8,128)(2,1)S(1)}, u32[]{:S(2)}, u32[]{:S(2)}) async-start(bf16[4,64,640]{2,1,0:T(8,128)(2,1)} %broadcast_in_dim.3), calls=%async_computation.2 | async-start | bytes 655360 | tf_op jit(solution)/shard_map/all_to_all | solution.py:191

commit v5 on v4

--- a/solution.py
+++ b/solution.py
@@ -47,12 +47,13 @@
         copy.wait()
     heads, depth, latent = key.shape
     rows = [key[:, :, c : c + 128].reshape(heads * depth, 128) for c in range(0, latent, 128)]
-    both = jnp.concatenate(rows + [value[...].reshape(-1, 128)], 0)
-    for i in range(out_ref.shape[0]):
-        out_ref[i] = both
-
-
-def absorb_kernel(heads, latent, parts_ref, nope_ref, rope_ref, out_ref):
+    keys = jnp.concatenate(rows, 0)
+    for i, member in enumerate(order("batch", out_ref.shape[0])):
+        out_ref[i] = jnp.concatenate([keys, value[member % heads]], 0)
+
+
+def absorb_kernel(heads, latent, parts_ref, nope_ref, rope_ref, out_ref, values_ref):
+    values_ref[...] = parts_ref[:, parts_ref.shape[1] - values_ref.shape[1] :]
     tokens = nope_ref.shape[1]
     head_width = nope_ref.shape[2] // heads
     rope_width = rope_ref.shape[2] // heads
@@ -100,8 +101,9 @@
 
 def combined(latent, sums_ref):
     stats = sums_ref[:, :, latent:].astype(F32)
-    peak = stats[:, :, 0:1] + stats[:, :, 1:2] + stats[:, :, 2:3]
-    total = stats[:, :, 3:4] + stats[:, :, 4:5] + stats[:, :, 5:6]
+    lane = lax.broadcasted_iota(jnp.int32, stats.shape, 2)
+    peak = jnp.sum(jnp.where(lane < 3, stats, 0.0), axis=2, keepdims=True)
+    total = jnp.sum(jnp.where(lane < 3, 0.0, stats), axis=2, keepdims=True)
     top = jnp.max(peak, axis=0)
     factor = jnp.exp(peak - top[None])
     total = jnp.sum(factor * total, axis=0)
@@ -142,25 +144,14 @@
         out_ref[i] = out[i * rows : (i + 1) * rows].astype(BF16)
 
 
-def combine_kernel(heads, tokens, latent, sums_ref, parts_ref, out_ref):
+def combine_kernel(heads, tokens, latent, sums_ref, own_ref, other_ref, out_ref):
     summed, _, total = combined(latent, sums_ref)
     mixed = (summed / total).astype(BF16)
-    groups, rows = parts_ref.shape[0], parts_ref.shape[1]
-    depth = latent // groups
-    first = rows - heads * depth
-    values = jnp.concatenate(
-        [
-            jnp.concatenate(
-                [
-                    parts_ref[place, first + h * depth : first + (h + 1) * depth]
-                    for place in places(groups)
-                ],
-                0,
-            )
-            for h in range(heads)
-        ],
-        1,
-    )
+    groups = own_ref.shape[0]
+    own = jnp.concatenate([own_ref[place] for place in places(groups)], 0)
+    other = jnp.concatenate([other_ref[place] for place in places(groups)], 0)
+    second = lax.axis_index("batch") % 2 == 1
+    values = jnp.concatenate([jnp.where(second, other, own), jnp.where(second, own, other)], 1)
     out = jnp.dot(mixed, values, preferred_element_type=F32)
     for t in range(tokens):
         for h in range(heads):
@@ -199,7 +190,7 @@
     rope_width = query_rope.shape[2] // heads
     own = tokens * heads
     wide = latent + 128
-    part_rows = (key_up.size + value_up.size) // 128
+    part_rows = (key_up.size + value_up.size // heads) // 128
     like = jax.ShapeDtypeStruct
     copies, nope, rope = pl.pallas_call(
         pack_kernel,
@@ -222,10 +213,22 @@
     ])
     parts = exchange(copies, "batch")
     absorb = functools.partial(absorb_kernel, heads, latent)
-    queries = call(absorb, (high, own, wide), 3)(parts, nope, rope)
+    queries, values = pl.pallas_call(
+        absorb,
+        out_shape=(
+            like((high, own, wide), BF16),
+            like((groups, latent // groups, 128), BF16),
+        ),
+        in_specs=[VMEM] * 3,
+        out_specs=[VMEM] * 2,
+        compiler_params=PARAMS,
+    )(parts, nope, rope)
     queries = exchange(queries, "z")
+    values, queries = lax.optimization_barrier((values, queries))
     queries = jnp.broadcast_to(queries.reshape(high * own, wide), (low, high * own, wide))
     queries = exchange(queries, "y")
+    other = lax.ppermute(values, "batch", [(i, i ^ 1) for i in range(groups)])
+    other, queries = lax.optimization_barrier((other, queries))
     scale = 1.0 / math.sqrt(head_width + rope_width)
     attend = functools.partial(attend_kernel, heads, tokens, scale, latent)
     sums = call(attend, (low * high * own, wide), 3, [VMEM, VMEM, pl.BlockSpec(memory_space=pltpu.SMEM)])(
@@ -235,7 +238,7 @@
     sums = call(functools.partial(add_kernel, latent), (high, own, wide), 1)(sums)
     sums = exchange(sums, "z")
     combine = functools.partial(combine_kernel, heads, tokens, latent)
-    return call(combine, (1, tokens, heads * 128), 2)(sums, parts)
+    return call(combine, (1, tokens, heads * 128), 3)(sums, values, other)
 
 
 Y_SIZE = 4

time: 75.5 us -> 74.2 us (0.983)
  the two profiles are of different devices: /device:TPU:4 before, /device:TPU:2 now
where the time goes in v5:
time: 74.2 us; the launch traced here: 73.8 us
  blocking collectives  58.9 us (79%)
  starting transfers between devices  8.52 us (11%)
  Pallas kernels  3.15 us (4%)
  waiting for transfers between devices  1.74 us (2%)
  local copies, waits for them, and re-layouts  0.78 us (1%)
    all_to_all x4, blocking collectives, exchange(): lax.all_to_all(blocks, axis, 0, 0, axis_index_groups=groups, tiled=True)  58.9 us
    all_to_all x1, starting transfers between devices, exchange(): lax.all_to_all(blocks, axis, 0, 0, axis_index_groups=groups, tiled=True)  6.62 us
    ppermute x1, starting transfers between devices, body(): other = lax.ppermute(values, 'batch', [(i, i ^ 1) for i in range(groups)])  1.91 us
  transfers between devices with their start and end apart: 2, of which 2 were waited for; matrix products, arithmetic and copies ran while one was open for 0% of the time, Pallas kernels for 0%

profile of v5, /device:TPU:2, one launch (start us, length us, event | category | flops | bytes accessed | tf_op | source)
XLA Modules:
  0.0 73.8 jit_solution(1946973932806209703)
XLA Ops:
  0.0 0.9 %shard_map.64 = (bf16[8,192,128]{2,1,0:T(8,128)(2,1)S(1)}, bf16[1,2,256]{2,1,0:T(2,128)(2,1)S(1)}, bf16[1,2,128]{2,1,0:T(2,128)(2,1)S(1)}) custom-call(bf16[2,16,512]{2,1,0:T(8,128)(2,1)} %key_ref.1, bf16[2,64,128]{2,1,0:T(8,128)(2,1)} %value_ref.1, bf16[1,2,256]{2,1,0:T(2,128)(2,1)} %nope_ref.1, bf16[1,2,128]{2,1,0:T(2,128)(2,1)} %rope_ref.1), custom_call_target="tpu_custom_call" | custom-call | tf_op jit(solution)/shard_map/pallas_call | solution.py:195
  0.9 0.0 copy-start
  0.9 15.4 %all_to_all.25.parts_ref = bf16[8,192,128]{2,1,0:T(8,128)(2,1)S(1)} all-to-all(bf16[8,192,128]{2,1,0:T(8,128)(2,1)S(1)} %get-tuple-element.14), channel_id=1, replica_groups={{320,384,448,0,64,128,192,256},{321,385,449,1,65,129,193,257},{322,386,..., dimensions={0} | all-to-all | bytes 786432 | tf_op jit(solution)/shard_map/all_to_all | solution.py:182
  16.3 0.2 shard_map.65
  16.5 18.4 %all_to_all.26 = bf16[16,4,640]{2,1,0:T(4,128)(2,1)S(1)} all-to-all(bf16[16,4,640]{2,1,0:T(4,128)(2,1)S(1)} %get-tuple-element.18), channel_id=1, replica_groups={{32,36,40,44,48,52,56,60,0,4,8,12,16,20,24,28},{33,37,41,45,49,53,57,61..., dimensions={0} | all-to-all | bytes 163840 | tf_op jit(solution)/shard_map/all_to_all | solution.py:182
  34.9 0.8 %broadcast_in_dim.3 = bf16[4,64,640]{2,1,0:T(8,128)(2,1)} broadcast(bf16[64,640]{1,0:T(8,128)(2,1)S(1)} %reshape.9), dimensions={1,2} | broadcast | bytes 409600 | tf_op jit(solution)/shard_map/broadcast_in_dim | solution.py:228
  35.6 6.6 %all-to-all-start.2 = ((bf16[4,64,640]{2,1,0:T(8,128)(2,1)}), bf16[4,64,640]{2,1,0:T(8,128)(2,1)S(1)}, u32[]{:S(2)}, u32[]{:S(2)}) async-start(bf16[4,64,640]{2,1,0:T(8,128)(2,1)} %broadcast_in_dim.3), calls=%async_computation.2 | async-start | bytes 655360 | tf_op jit(solution)/shard_map/all_to_all | solution.py:182
  42.2 1.9 %collective-permute-start = (bf16[8,64,128]{2,1,0:T(8,128)(2,1)S(1)}, bf16[8,64,128]{2,1,0:T(8,128)(2,1)S(1)}, u32[]{:S(2)}, u32[]{:S(2)}) collective-permute-start(bf16[8,64,128]{2,1,0:T(8,128)(2,1)S(1)} %get-tuple-element.19.own_ref), channel_id=1, source_target_pairs={{0,64},{64,0},{128,192},{192,128},{256,320},{320,256},{384,448},{4... | collective-permute-start | bytes 393224 | tf_op jit(solution)/shard_map/ppermute | solution.py:230
  44.8 0.7 collective-permute-done.other_ref
  45.5 1.1 %all-to-all-done.2 = bf16[4,64,640]{2,1,0:T(8,128)(2,1)S(1)} async-done(((bf16[4,64,640]{2,1,0:T(8,128)(2,1)}), bf16[4,64,640]{2,1,0:T(8,128)(2,1)S(1)}, u32[]{:S(2)}, u32[]{:S(2)}) %all-to-all-start.2) | async-done | bytes 327712 | tf_op jit(solution)/shard_map/all_to_all | solution.py:182
  46.5 0.0 copy-done
  46.6 1.1 %shard_map.66 = bf16[256,640]{1,0:T(8,128)(2,1)S(1)} custom-call(bf16[256,640]{1,0:T(8,128)(2,1)S(1)} %bitcast.5, bf16[576,1024]{1,0:T(8,128)(2,1)S(1)} %bitcast.7, s32[1]{0:T(128)S(6)} %copy.7.length_ref), custom_call_target="tpu_custom_call" | custom-call | tf_op jit(solution)/shard_map/pallas_call | solution.py:234
  47.6 9.2 %all_to_all.27.sums_ref = bf16[4,64,640]{2,1,0:T(8,128)(2,1)S(1)} all-to-all(bf16[4,64,640]{2,1,0:T(8,128)(2,1)S(1)} %bitcast.6), channel_id=1, replica_groups={{2,3,0,1},{6,7,4,5},{10,11,8,9},{14,15,12,13},{18,19,16,17},{22,23,20,2..., dimensions={0} | all-to-all | bytes 655360 | tf_op jit(solution)/shard_map/all_to_all | solution.py:182
  56.9 0.2 shard_map.67
  57.1 15.9 %all_to_all.28.sums_ref = bf16[16,4,640]{2,1,0:T(4,128)(2,1)S(1)} all-to-all(bf16[16,4,640]{2,1,0:T(4,128)(2,1)S(1)} %shard_map.67), channel_id=1, replica_groups={{32,36,40,44,48,52,56,60,0,4,8,12,16,20,24,28},{33,37,41,45,49,53,57,61..., dimensions={0} | all-to-all | bytes 163840 | tf_op jit(solution)/shard_map/all_to_all | solution.py:182
  73.0 0.8 %shard_map.68 = bf16[1,2,256]{2,1,0:T(2,128)(2,1)} custom-call(bf16[16,4,640]{2,1,0:T(4,128)(2,1)S(1)} %all_to_all.28.sums_ref, bf16[8,64,128]{2,1,0:T(8,128)(2,1)S(1)} %get-tuple-element.19.own_ref, bf16[8,64,128]{2,1,0:T(8,128)(2,1)S(1)} %collective-permute-done.other_ref), custom_call_target="tpu_custom_call" | custom-call | tf_op jit(solution)/shard_map/pallas_call | solution.py:241
  (1 shorter events, 0.0 us)
Async XLA Ops:
  0.9 45.7 %copy-start = (bf16[1,1024,576]{1,2,0:T(8,128)(2,1)S(1)}, bf16[1,1024,576]{1,2,0:T(8,128)(2,1)}, u32[]{:S(2)}) copy-start(bf16[1,1024,576]{1,2,0:T(8,128)(2,1)} %param.8) | copy-start | bytes 3538948
  35.6 10.9 %all-to-all-start.2 = ((bf16[4,64,640]{2,1,0:T(8,128)(2,1)}), bf16[4,64,640]{2,1,0:T(8,128)(2,1)S(1)}, u32[]{:S(2)}, u32[]{:S(2)}) async-start(bf16[4,64,640]{2,1,0:T(8,128)(2,1)} %broadcast_in_dim.3), calls=%async_computation.2 | async-start | bytes 655360 | tf_op jit(solution)/shard_map/all_to_all | solution.py:182
  42.2 3.2 %collective-permute-start = (bf16[8,64,128]{2,1,0:T(8,128)(2,1)S(1)}, bf16[8,64,128]{2,1,0:T(8,128)(2,1)S(1)}, u32[]{:S(2)}, u32[]{:S(2)}) collective-permute-start(bf16[8,64,128]{2,1,0:T(8,128)(2,1)S(1)} %get-tuple-element.19.own_ref), channel_id=1, source_target_pairs={{0,64},{64,0},{128,192},{192,128},{256,320},{320,256},{384,448},{4... | collective-permute-start | bytes 393224 | tf_op jit(solution)/shard_map/ppermute | solution.py:230

commit v6 on v5

--- a/solution.py
+++ b/solution.py
@@ -43,13 +43,18 @@
     ]
     for copy in copies:
         copy.start()
-    for copy in copies:
-        copy.wait()
+    copies[0].wait()
     heads, depth, latent = key.shape
     rows = [key[:, :, c : c + 128].reshape(heads * depth, 128) for c in range(0, latent, 128)]
     keys = jnp.concatenate(rows, 0)
-    for i, member in enumerate(order("batch", out_ref.shape[0])):
-        out_ref[i] = jnp.concatenate([keys, value[member % heads]], 0)
+    members = order("batch", out_ref.shape[0])
+    for i in range(len(members)):
+        out_ref[i, : keys.shape[0]] = keys
+    copies[1].wait()
+    for i, member in enumerate(members):
+        out_ref[i, keys.shape[0] :] = value[member % heads]
+    for copy in copies[2:]:
+        copy.wait()
 
 
 def absorb_kernel(heads, latent, parts_ref, nope_ref, rope_ref, out_ref, values_ref):

time: 74.2 us -> 74.2 us (level)
  no operation moved by 1% of the time
where the time goes in v6:
time: 74.2 us; the launch traced here: 73.8 us
  blocking collectives  58.9 us (79%)
  starting transfers between devices  8.52 us (11%)
  Pallas kernels  3.13 us (4%)
  waiting for transfers between devices  1.74 us (2%)
  local copies, waits for them, and re-layouts  0.78 us (1%)
    all_to_all x4, blocking collectives, exchange(): lax.all_to_all(blocks, axis, 0, 0, axis_index_groups=groups, tiled=True)  58.9 us
    all_to_all x1, starting transfers between devices, exchange(): lax.all_to_all(blocks, axis, 0, 0, axis_index_groups=groups, tiled=True)  6.62 us
    ppermute x1, starting transfers between devices, body(): other = lax.ppermute(values, 'batch', [(i, i ^ 1) for i in range(groups)])  1.91 us
  transfers between devices with their start and end apart: 2, of which 2 were waited for; matrix products, arithmetic and copies ran while one was open for 0% of the time, Pallas kernels for 0%

profile of v6, /device:TPU:2, one launch (start us, length us, event | category | flops | bytes accessed | tf_op | source)
XLA Modules:
  0.0 73.8 jit_solution(13475868582633947435)
XLA Ops:
  0.0 0.8 %shard_map.64 = (bf16[8,192,128]{2,1,0:T(8,128)(2,1)S(1)}, bf16[1,2,256]{2,1,0:T(2,128)(2,1)S(1)}, bf16[1,2,128]{2,1,0:T(2,128)(2,1)S(1)}) custom-call(bf16[2,16,512]{2,1,0:T(8,128)(2,1)} %key_ref.1, bf16[2,64,128]{2,1,0:T(8,128)(2,1)} %value_ref.1, bf16[1,2,256]{2,1,0:T(2,128)(2,1)} %nope_ref.1, bf16[1,2,128]{2,1,0:T(2,128)(2,1)} %rope_ref.1), custom_call_target="tpu_custom_call" | custom-call | tf_op jit(solution)/shard_map/pallas_call | solution.py:200
  0.9 0.0 copy-start
  0.9 15.4 %all_to_all.25.parts_ref = bf16[8,192,128]{2,1,0:T(8,128)(2,1)S(1)} all-to-all(bf16[8,192,128]{2,1,0:T(8,128)(2,1)S(1)} %get-tuple-element.14), channel_id=1, replica_groups={{320,384,448,0,64,128,192,256},{321,385,449,1,65,129,193,257},{322,386,..., dimensions={0} | all-to-all | bytes 786432 | tf_op jit(solution)/shard_map/all_to_all | solution.py:187
  16.3 0.2 shard_map.65
  16.5 18.4 %all_to_all.26 = bf16[16,4,640]{2,1,0:T(4,128)(2,1)S(1)} all-to-all(bf16[16,4,640]{2,1,0:T(4,128)(2,1)S(1)} %get-tuple-element.18), channel_id=1, replica_groups={{32,36,40,44,48,52,56,60,0,4,8,12,16,20,24,28},{33,37,41,45,49,53,57,61..., dimensions={0} | all-to-all | bytes 163840 | tf_op jit(solution)/shard_map/all_to_all | solution.py:187
  34.9 0.8 %broadcast_in_dim.3 = bf16[4,64,640]{2,1,0:T(8,128)(2,1)} broadcast(bf16[64,640]{1,0:T(8,128)(2,1)S(1)} %reshape.9), dimensions={1,2} | broadcast | bytes 409600 | tf_op jit(solution)/shard_map/broadcast_in_dim | solution.py:233
  35.6 6.6 %all-to-all-start.2 = ((bf16[4,64,640]{2,1,0:T(8,128)(2,1)}), bf16[4,64,640]{2,1,0:T(8,128)(2,1)S(1)}, u32[]{:S(2)}, u32[]{:S(2)}) async-start(bf16[4,64,640]{2,1,0:T(8,128)(2,1)} %broadcast_in_dim.3), calls=%async_computation.2 | async-start | bytes 655360 | tf_op jit(solution)/shard_map/all_to_all | solution.py:187
  42.2 1.9 %collective-permute-start = (bf16[8,64,128]{2,1,0:T(8,128)(2,1)S(1)}, bf16[8,64,128]{2,1,0:T(8,128)(2,1)S(1)}, u32[]{:S(2)}, u32[]{:S(2)}) collective-permute-start(bf16[8,64,128]{2,1,0:T(8,128)(2,1)S(1)} %get-tuple-element.19.own_ref), channel_id=1, source_target_pairs={{0,64},{64,0},{128,192},{192,128},{256,320},{320,256},{384,448},{4... | collective-permute-start | bytes 393224 | tf_op jit(solution)/shard_map/ppermute | solution.py:235
  44.8 0.7 collective-permute-done.other_ref
  45.5 1.1 %all-to-all-done.2 = bf16[4,64,640]{2,1,0:T(8,128)(2,1)S(1)} async-done(((bf16[4,64,640]{2,1,0:T(8,128)(2,1)}), bf16[4,64,640]{2,1,0:T(8,128)(2,1)S(1)}, u32[]{:S(2)}, u32[]{:S(2)}) %all-to-all-start.2) | async-done | bytes 327712 | tf_op jit(solution)/shard_map/all_to_all | solution.py:187
  46.5 0.0 copy-done
  46.5 1.1 %shard_map.66 = bf16[256,640]{1,0:T(8,128)(2,1)S(1)} custom-call(bf16[256,640]{1,0:T(8,128)(2,1)S(1)} %bitcast.5, bf16[576,1024]{1,0:T(8,128)(2,1)S(1)} %bitcast.7, s32[1]{0:T(128)S(6)} %copy.7.length_ref), custom_call_target="tpu_custom_call" | custom-call | tf_op jit(solution)/shard_map/pallas_call | solution.py:239
  47.6 9.2 %all_to_all.27.sums_ref = bf16[4,64,640]{2,1,0:T(8,128)(2,1)S(1)} all-to-all(bf16[4,64,640]{2,1,0:T(8,128)(2,1)S(1)} %bitcast.6), channel_id=1, replica_groups={{2,3,0,1},{6,7,4,5},{10,11,8,9},{14,15,12,13},{18,19,16,17},{22,23,20,2..., dimensions={0} | all-to-all | bytes 655360 | tf_op jit(solution)/shard_map/all_to_all | solution.py:187
  56.8 0.2 shard_map.67
  57.0 15.9 %all_to_all.28.sums_ref = bf16[16,4,640]{2,1,0:T(4,128)(2,1)S(1)} all-to-all(bf16[16,4,640]{2,1,0:T(4,128)(2,1)S(1)} %shard_map.67), channel_id=1, replica_groups={{32,36,40,44,48,52,56,60,0,4,8,12,16,20,24,28},{33,37,41,45,49,53,57,61..., dimensions={0} | all-to-all | bytes 163840 | tf_op jit(solution)/shard_map/all_to_all | solution.py:187
  72.9 0.8 %shard_map.68 = bf16[1,2,256]{2,1,0:T(2,128)(2,1)} custom-call(bf16[16,4,640]{2,1,0:T(4,128)(2,1)S(1)} %all_to_all.28.sums_ref, bf16[8,64,128]{2,1,0:T(8,128)(2,1)S(1)} %get-tuple-element.19.own_ref, bf16[8,64,128]{2,1,0:T(8,128)(2,1)S(1)} %collective-permute-done.other_ref), custom_call_target="tpu_custom_call" | custom-call | tf_op jit(solution)/shard_map/pallas_call | solution.py:246
  (1 shorter events, 0.0 us)
Async XLA Ops:
  0.9 45.7 %copy-start = (bf16[1,1024,576]{1,2,0:T(8,128)(2,1)S(1)}, bf16[1,1024,576]{1,2,0:T(8,128)(2,1)}, u32[]{:S(2)}) copy-start(bf16[1,1024,576]{1,2,0:T(8,128)(2,1)} %param.8) | copy-start | bytes 3538948
  35.6 10.9 %all-to-all-start.2 = ((bf16[4,64,640]{2,1,0:T(8,128)(2,1)}), bf16[4,64,640]{2,1,0:T(8,128)(2,1)S(1)}, u32[]{:S(2)}, u32[]{:S(2)}) async-start(bf16[4,64,640]{2,1,0:T(8,128)(2,1)} %broadcast_in_dim.3), calls=%async_computation.2 | async-start | bytes 655360 | tf_op jit(solution)/shard_map/all_to_all | solution.py:187
  42.2 3.2 %collective-permute-start = (bf16[8,64,128]{2,1,0:T(8,128)(2,1)S(1)}, bf16[8,64,128]{2,1,0:T(8,128)(2,1)S(1)}, u32[]{:S(2)}, u32[]{:S(2)}) collective-permute-start(bf16[8,64,128]{2,1,0:T(8,128)(2,1)S(1)} %get-tuple-element.19.own_ref), channel_id=1, source_target_pairs={{0,64},{64,0},{128,192},{192,128},{256,320},{320,256},{384,448},{4... | collective-permute-start | bytes 393224 | tf_op jit(solution)/shard_map/ppermute | solution.py:235
